TPU v7x, 256 devices: a whole 4x4x8 slice. The times are simulated.
256 devices in a mesh: store: 32 (over z, y), tp: 8 (over x, core).
Axes of the slice: x: 4, y: 4, z: 8, core: 2. Of those that a mesh axis runs over, the one named last changes fastest.
Arguments:
- query: bfloat16 [2560, 8192], P('store', 'tp')
- new_kv: bfloat16 [2, 2560, 1024], P(None, 'store', 'tp')
- kv_store: bfloat16 [2, 640, 512, 1024], P(None, 'store', None, 'tp'), may hold values from -6 to 6
- passage_ids: int32 [256, 10], P('store'), may hold values from 0 to 639, as said below
- residual_in: bfloat16 [2560, 8192], P('store', 'tp'), may hold values from -3 to 3
- out_weight: bfloat16 [8192, 8192], P('tp', 'store'), may hold values from -0.75 to 0.75
Outputs:
- layer_out: bfloat16 [2560, 8192], P('store', 'tp')
Inputs may be any that keep to these rules, and one draw needn't show every extreme that they name: `passage_ids`: store shard s holds passages s * 20 to (s + 1) * 20 - 1. In each aligned block of 8 rows (the queries of one index of store), every shard that is named at all is named exactly 5 times; popular shards are named in more blocks and low passage numbers within a shard are more popular.
All inputs are finite; a program needn't handle non-finite values.
Results may differ from a plain program's by a relative error of at most 0.018.
Values may be sent and summed in bfloat16 or wider, within the bound.
A program may use at most 64 MiB of HBM per device.

v0:
```python
import jax
import jax.numpy as jnp
from jax import lax
from jax.sharding import PartitionSpec as P

H = 64
KVH = 8
HD = 128
PLEN = 512


def attend_slots(queries, own_pairs, passage_local, kv_store):
    slot_count = queries.shape[0]
    kv_width = own_pairs.shape[1] // 2
    kv_heads = kv_width // HD
    group_size = H // KVH
    scaling = 1.0 / HD**0.5
    pass_local = kv_store.shape[1]
    query_heads = queries.reshape(slot_count, kv_heads, group_size, HD)
    own_keys = own_pairs[:, :kv_width].reshape(slot_count, kv_heads, HD)
    own_values = own_pairs[:, kv_width:].reshape(slot_count, kv_heads, HD)
    own_score = (
        jnp.einsum("bgjd,bgd->bgj", query_heads, own_keys, preferred_element_type=jnp.float32)
        * scaling
    )
    own_float = own_values.astype(jnp.float32)[:, :, None, :]

    def one_passage(index, result):
        block = lax.dynamic_index_in_dim(kv_store, index, 1, keepdims=False)
        stored_keys = block[0].reshape(PLEN, kv_heads, HD)
        stored_values = block[1].reshape(PLEN, kv_heads, HD)
        scores = (
            jnp.einsum(
                "bgjd,kgd->bgjk", query_heads, stored_keys, preferred_element_type=jnp.float32
            )
            * scaling
        )
        highest = jnp.maximum(jnp.max(scores, axis=-1), own_score)
        exponent_terms = jnp.exp(scores - highest[..., None])
        own_term = jnp.exp(own_score - highest)
        totals = jnp.sum(exponent_terms, axis=-1) + own_term
        weights = (exponent_terms / totals[..., None]).astype(jnp.bfloat16)
        own_weight = (own_term / totals).astype(jnp.bfloat16)
        mixed = jnp.einsum(
            "bgjk,kgd->bgjd", weights, stored_values, preferred_element_type=jnp.float32
        )
        mixed = (mixed + own_weight.astype(jnp.float32)[..., None] * own_float).astype(jnp.bfloat16)
        matching = (passage_local == index)[:, None, None, None]
        return jnp.where(matching, mixed, result)

    start = jnp.zeros((slot_count, kv_heads, group_size, HD), jnp.bfloat16)
    result = lax.fori_loop(0, pass_local, one_passage, start)
    return result.reshape(slot_count, kv_heads * group_size * HD)


def shards(query, new_kv, kv_store, passage_ids, residual_in, out_weight):
    store_count = lax.axis_size("store")
    local_streams = query.shape[0]
    head_width = query.shape[1]
    kv_width = new_kv.shape[2]
    pass_local = kv_store.shape[1]
    fan_out = min(store_count, 16)
    per_shard = local_streams // fan_out
    slots_total = store_count * per_shard
    stream_passages = passage_ids.reshape(local_streams)
    owner_shard = stream_passages // pass_local
    local_passage = stream_passages - owner_shard * pass_local
    owner_onehot = (owner_shard[:, None] == jnp.arange(store_count)[None, :]).astype(jnp.int32)
    earlier = jnp.cumsum(owner_onehot, axis=0) - owner_onehot
    position = jnp.sum(earlier * owner_onehot, axis=1)
    slot_index = owner_shard * per_shard + position
    slot_match = jnp.arange(slots_total)[:, None] == slot_index[None, :]
    selector = slot_match.astype(jnp.bfloat16)
    gatherer = (slot_index[:, None] == jnp.arange(slots_total)[None, :]).astype(jnp.bfloat16)
    own_pairs = jnp.concatenate([new_kv[0], new_kv[1]], axis=1)
    send_queries = jnp.dot(selector, query, preferred_element_type=jnp.float32).astype(jnp.bfloat16)
    send_pairs = jnp.dot(selector, own_pairs, preferred_element_type=jnp.float32).astype(
        jnp.bfloat16
    )
    send_local = jnp.sum(jnp.where(slot_match, local_passage[None, :], 0), axis=1)
    send_queries = send_queries.reshape(store_count, per_shard, head_width)
    send_pairs = send_pairs.reshape(store_count, per_shard, 2 * kv_width)
    send_local = send_local.reshape(store_count, per_shard)
    recv_queries = lax.all_to_all(send_queries, "store", split_axis=0, concat_axis=0, tiled=True)
    recv_pairs = lax.all_to_all(send_pairs, "store", split_axis=0, concat_axis=0, tiled=True)
    recv_local = lax.all_to_all(send_local, "store", split_axis=0, concat_axis=0, tiled=True)
    sources = recv_queries.shape[0]
    per_source = recv_queries.shape[1]
    results = attend_slots(
        recv_queries.reshape(sources * per_source, head_width),
        recv_pairs.reshape(sources * per_source, 2 * kv_width),
        recv_local.reshape(sources * per_source),
        kv_store,
    )
    results = results.reshape(sources, per_source, head_width)
    returned = lax.all_to_all(results, "store", split_axis=0, concat_axis=0, tiled=True)
    attention = jnp.dot(
        gatherer, returned.reshape(slots_total, head_width), preferred_element_type=jnp.float32
    ).astype(jnp.bfloat16)
    partial_full = jnp.dot(
        attention,
        lax.all_gather(out_weight, "store", axis=1, tiled=True),
        preferred_element_type=jnp.float32,
    )
    projected = lax.psum_scatter(
        partial_full.astype(jnp.bfloat16), "tp", scatter_dimension=1, tiled=True
    ).astype(jnp.float32)
    return (residual_in.astype(jnp.float32) + projected).astype(jnp.bfloat16)


def solution(mesh):
    placed = (
        P("store", "tp"),
        P(None, "store", "tp"),
        P(None, "store", None, "tp"),
        P("store", None),
        P("store", "tp"),
        P("tp", "store"),
    )
    return jax.shard_map(
        shards, mesh=mesh, in_specs=placed, out_specs=P("store", "tp"), check_vma=False
    )
```

profile of v0, /device:TPU:8, one launch (start us, length us, event | category | flops | bytes accessed | tf_op | source)
XLA Modules:
  0.0 264.2 jit_solution(4640889365879576970)
XLA Ops:
  8.6 11.7 %all-to-all-start = ((s32[32,1,5]{2,1,0:T(1,128)}), s32[32,1,5]{2,1,0:T(1,128)S(1)}, u32[]{:S(2)}, u32[]{:S(2)}) async-start(s32[32,1,5]{2,1,0:T(1,128)} %bitcast), calls=%async_computation | async-start | bytes 32768 | tf_op jit(solution)/shard_map/all_to_all | solution.py:86
  21.9 6.9 %all-to-all-done = s32[32,1,5]{2,1,0:T(1,128)S(1)} async-done(((s32[32,1,5]{2,1,0:T(1,128)}), s32[32,1,5]{2,1,0:T(1,128)S(1)}, u32[]{:S(2)}, u32[]{:S(2)}) %all-to-all-start) | async-done | bytes 672 | tf_op jit(solution)/shard_map/all_to_all | solution.py:86
  28.8 4.8 %all-to-all-start.2 = ((bf16[32,5,256]{2,1,0:T(8,128)(2,1)}), bf16[32,5,256]{2,1,0:T(8,128)(2,1)S(1)}, u32[]{:S(2)}, u32[]{:S(2)}) async-start(bf16[32,5,256]{2,1,0:T(8,128)(2,1)} %reshape.233), calls=%async_computation.2 | async-start | bytes 262144 | tf_op jit(solution)/shard_map/all_to_all | solution.py:85
  33.9 0.9 reshape.231
  34.8 7.8 %all-to-all-done.2 = bf16[32,5,256]{2,1,0:T(8,128)(2,1)S(1)} async-done(((bf16[32,5,256]{2,1,0:T(8,128)(2,1)}), bf16[32,5,256]{2,1,0:T(8,128)(2,1)S(1)}, u32[]{:S(2)}, u32[]{:S(2)}) %all-to-all-start.2) | async-done | bytes 81952 | tf_op jit(solution)/shard_map/all_to_all | solution.py:85
  42.6 5.5 %all-to-all-start.1 = ((bf16[32,5,1024]{2,1,0:T(8,128)(2,1)}), bf16[32,5,1024]{2,1,0:T(8,128)(2,1)S(1)}, u32[]{:S(2)}, u32[]{:S(2)}) async-start(bf16[32,5,1024]{2,1,0:T(8,128)(2,1)} %reshape.231), calls=%async_computation.1 | async-start | bytes 1048576 | tf_op jit(solution)/shard_map/all_to_all | solution.py:84
  50.8 12.1 %all-to-all-done.1 = bf16[32,5,1024]{2,1,0:T(8,128)(2,1)S(1)} async-done(((bf16[32,5,1024]{2,1,0:T(8,128)(2,1)}), bf16[32,5,1024]{2,1,0:T(8,128)(2,1)S(1)}, u32[]{:S(2)}, u32[]{:S(2)}) %all-to-all-start.1) | async-done | bytes 327712 | tf_op jit(solution)/shard_map/all_to_all | solution.py:84
  64.1 101.1 %while.14 = (s32[]{:T(128)}, bf16[160,1,8,128]{3,0,2,1:T(8,128)(2,1)S(1)}, s32[160]{0:T(256)}, bf16[2,20,512,128]{3,2,1,0:T(8,128)(2,1)}, bf16[160,1,8,128]{3,0,...) while((s32[]{:T(128)}, ...), condition=%wide.region_6.7_spmd.clone, body=%wide.region_3.6_spmd.clone.sunk | while | flops 342268320 | bytes 9268159 | solution.py:52
  64.1 1.5 bitcast_reduce_fusion.2
  65.7 0.9 fusion.47
  67.2 2.0 fusion.49
  69.2 1.5 bitcast_reduce_fusion.2
  70.7 0.9 fusion.47
  72.2 2.0 fusion.49
  74.3 1.5 bitcast_reduce_fusion.2
  75.8 0.9 fusion.47
  77.3 2.0 fusion.49
  79.3 1.5 bitcast_reduce_fusion.2
  80.8 0.9 fusion.47
  82.3 2.0 fusion.49
  84.4 1.5 bitcast_reduce_fusion.2
  85.9 0.9 fusion.47
  87.4 2.0 fusion.49
  89.4 1.5 bitcast_reduce_fusion.2
  90.9 0.9 fusion.47
  92.4 2.0 fusion.49
  94.5 1.5 bitcast_reduce_fusion.2
  96.0 0.9 fusion.47
  97.5 2.0 fusion.49
  99.5 1.5 bitcast_reduce_fusion.2
  101.0 0.9 fusion.47
  102.5 2.0 fusion.49
  104.6 1.5 bitcast_reduce_fusion.2
  106.1 0.9 fusion.47
  107.6 2.0 fusion.49
  109.6 1.5 bitcast_reduce_fusion.2
  112.6 2.0 fusion.49
  114.7 1.5 bitcast_reduce_fusion.2
  117.7 2.0 fusion.49
  119.7 1.5 bitcast_reduce_fusion.2
  122.7 2.0 fusion.49
  124.8 1.5 bitcast_reduce_fusion.2
  127.8 2.0 fusion.49
  129.8 1.5 bitcast_reduce_fusion.2
  132.8 2.0 fusion.49
  134.9 1.5 bitcast_reduce_fusion.2
  137.9 2.0 fusion.49
  139.9 1.5 bitcast_reduce_fusion.2
  141.4 0.9 fusion.47
  142.9 2.0 fusion.49
  145.0 1.5 bitcast_reduce_fusion.2
  148.0 2.0 fusion.49
  150.0 1.5 bitcast_reduce_fusion.2
  153.0 2.0 fusion.49
  155.1 1.5 bitcast_reduce_fusion.2
  158.1 2.0 fusion.49
  160.1 1.5 bitcast_reduce_fusion.2
  161.7 0.9 fusion.47
  163.1 2.0 fusion.49
  165.7 25.8 %all_to_all.24 = bf16[32,5,1024]{2,1,0:T(8,128)(2,1)S(1)} all-to-all(bf16[32,5,1024]{2,1,0:T(8,128)(2,1)S(1)} %reshape_reshape.7), channel_id=1, replica_groups=mesh['store'=32,'tp'=8] {'store'}, dimensions={0} | all-to-all | bytes 655360 | tf_op jit(solution)/shard_map/all_to_all | solution.py:96
  191.7 20.7 %all-gather.2.cloned.1.call-done = bf16[1024,8192]{1,0:T(8,128)(2,1)} async-done(((bf16[1024,256]{1,0:T(8,128)(2,1)}), bf16[1024,8192]{1,0:T(8,128)(2,1)}) %all-gather.2.cloned.1.call-update) | async-done | bytes 16777232 | tf_op jit(solution)/shard_map/all_gather | solution.py:102
  212.4 10.0 %convolution_convert_fusion = bf16[80,8192]{1,0:T(8,128)(2,1)} fusion(bf16[1024,8192]{1,0:T(8,128)(2,1)} %all-gather.2.cloned.1.call-done, bf16[160,1024]{1,0:T(8,128)(2,1)S(1)} %reshape.235, s32[80]{0:T(128)S(1)} %copy-done.4), kind=kOutput, calls=%fused_computation.26 | convolution fusion | flops 1369141760 | bytes 18415936 | tf_op jit(solution)/shard_map/dot_general | solution.py:100
  222.4 33.3 %reduce-scatter.2.cloned.1.call-done = bf16[80,1024]{1,0:T(8,128)(2,1)} async-done(((bf16[80,8192]{1,0:T(8,128)(2,1)}), bf16[80,1024]{1,0:T(8,128)(2,1)}) %reduce-scatter.2.cloned.1.call-update) | async-done | bytes 163856 | tf_op jit(solution)/shard_map/reduce_scatter | solution.py:105
  255.8 1.6 add_convert_fusion
  (148 shorter events, 28.0 us)
Async XLA Ops:
  6.5 27.1 %copy-start = (bf16[80,1024]{1,0:T(8,128)(2,1)S(1)}, bf16[80,1024]{1,0:T(8,128)(2,1)}, u32[]{:S(2)}) copy-start(bf16[80,1024]{1,0:T(8,128)(2,1)} %param.8) | copy-start | bytes 491524
  7.7 41.1 %copy-start.3 = (s32[80]{0:T(128)}, s32[80]{0:T(128)S(1)}, u32[]{:S(2)}) copy-start(s32[80]{0:T(128)S(1)} %multiply_add_fusion) | copy-start | bytes 964
  8.6 20.2 %all-to-all-start = ((s32[32,1,5]{2,1,0:T(1,128)}), s32[32,1,5]{2,1,0:T(1,128)S(1)}, u32[]{:S(2)}, u32[]{:S(2)}) async-start(s32[32,1,5]{2,1,0:T(1,128)} %bitcast), calls=%async_computation | async-start | bytes 32768 | tf_op jit(solution)/shard_map/all_to_all | solution.py:86
  28.8 13.8 %all-to-all-start.2 = ((bf16[32,5,256]{2,1,0:T(8,128)(2,1)}), bf16[32,5,256]{2,1,0:T(8,128)(2,1)S(1)}, u32[]{:S(2)}, u32[]{:S(2)}) async-start(bf16[32,5,256]{2,1,0:T(8,128)(2,1)} %reshape.233), calls=%async_computation.2 | async-start | bytes 262144 | tf_op jit(solution)/shard_map/all_to_all | solution.py:85
  42.6 20.3 %all-to-all-start.1 = ((bf16[32,5,1024]{2,1,0:T(8,128)(2,1)}), bf16[32,5,1024]{2,1,0:T(8,128)(2,1)S(1)}, u32[]{:S(2)}, u32[]{:S(2)}) async-start(bf16[32,5,1024]{2,1,0:T(8,128)(2,1)} %reshape.231), calls=%async_computation.1 | async-start | bytes 1048576 | tf_op jit(solution)/shard_map/all_to_all | solution.py:84
  48.1 164.3 %all-gather.2.cloned.1.call-start = ((), (), s32[]{:S(2)}) async-start(), calls=%async_computation.5 | async-start | bytes 17301504 | tf_op jit(solution)/shard_map/all_gather | solution.py:102
  48.8 207.0 %reduce-scatter.2.cloned.1.call-start = ((), (), s32[]{:S(2)}) async-start(), calls=%async_computation.6 | async-start | bytes 1474560 | tf_op jit(solution)/shard_map/reduce_scatter | solution.py:105
  64.1 2.5 copy-start.2
  69.2 2.5 copy-start.2
  74.2 2.5 copy-start.2
  79.3 2.5 copy-start.2
  84.4 2.5 copy-start.2
  89.4 2.5 copy-start.2
  94.4 2.5 copy-start.2
  99.5 2.5 copy-start.2
  104.6 2.5 copy-start.2
  109.6 2.5 copy-start.2
  114.7 2.5 copy-start.2
  119.7 2.5 copy-start.2
  124.8 2.5 copy-start.2
  129.8 2.5 copy-start.2
  134.9 2.5 copy-start.2
  139.9 2.5 copy-start.2
  145.0 2.5 copy-start.2
  150.0 2.5 copy-start.2
  155.1 2.5 copy-start.2
  160.1 2.5 copy-start.2
  165.2 47.2 %copy-start.4 = (s32[80]{0:T(128)S(1)}, s32[80]{0:T(128)}, u32[]{:S(2)}) copy-start(s32[80]{0:T(128)} %copy-done.3) | copy-start | bytes 964
  191.7 64.1 %copy-start.1 = (bf16[80,1024]{1,0:T(8,128)(2,1)S(1)}, bf16[80,1024]{1,0:T(8,128)(2,1)}, u32[]{:S(2)}) copy-start(bf16[80,1024]{1,0:T(8,128)(2,1)} %param.12) | copy-start | bytes 491524
Sparse Core Ops, SparseCore 0:
  51.4 160.9 all-gather.1
  222.5 33.1 reduce-scatter.1
where the time goes:
time: 265 us; the launch traced here: 264 us
  waiting for transfers between devices  81.5 us (31%)
  matrix products  81.3 us (31%)
  other arithmetic  32.2 us (12%)
  blocking collectives  25.8 us (10%)
  starting transfers between devices  22 us (8%)
  between operations  13.6 us (5%)
  local copies, waits for them, and re-layouts  6.82 us (3%)
    dot_general x20, matrix products, one_passage(): jnp.einsum('bgjk,kgd->bgjd', weights, stored_values, preferred_element_ty...  40.2 us
    reduce_scatter x1, waiting for transfers between devices, shards(): lax.psum_scatter(partial_full.astype(jnp.bfloat16), 'tp', scatter_dimensi...  33.3 us
    dot_general x20, matrix products, one_passage(): jnp.einsum('bgjd,kgd->bgjk', query_heads, stored_keys, preferred_element_...  30.4 us
    all_to_all x1, blocking collectives, shards(): lax.all_to_all(results, 'store', split_axis=0, concat_axis=0, tiled=True)  25.8 us
    all_gather x1, waiting for transfers between devices, shards(): lax.all_gather(out_weight, 'store', axis=1, tiled=True)  20.7 us
    reduce_sum x20, other arithmetic, one_passage(): totals = jnp.sum(exponent_terms, axis=-1) + own_term  18.1 us
    all_to_all x1, waiting for transfers between devices, shards(): lax.all_to_all(send_queries, 'store', split_axis=0, concat_axis=0, tiled=...  12.1 us
    all_to_all x1, starting transfers between devices, shards(): lax.all_to_all(send_local, 'store', split_axis=0, concat_axis=0, tiled=True)  11.7 us
  transfers between devices with their start and end apart: 5, of which 5 were waited for; matrix products, arithmetic and copies ran while one was open for 40% of the time, Pallas kernels for 0%

commit v1 on v0

v1 whole, which is shorter than its diff:
```python
import functools

import jax
import jax.numpy as jnp
import numpy as np
from jax import lax
from jax.experimental import pallas as pl
from jax.experimental.pallas import tpu as pltpu
from jax.sharding import PartitionSpec as P

HD = 128
PLEN = 512
GROUP = 8
SLOTS = 5
BLOCK = 16
WIDE = 3 * HD
PAD = 128
CHUNK = 16
Y_CHIPS = 4
MESH = pl.DeviceIdType.MESH
BF = jnp.bfloat16
F32 = jnp.float32
SCALE = 1.0 / HD**0.5
VMEM = pl.BlockSpec(memory_space=pltpu.VMEM)


def iota(shape, dim):
    return lax.broadcasted_iota(jnp.int32, shape, dim)


def dot(a, b):
    return jnp.dot(a, b, preferred_element_type=F32)


def row_parts(k):
    inner = jnp.bitwise_and(k, BLOCK - 1)
    group = (
        (inner >= SLOTS).astype(jnp.int32)
        + (inner >= 2 * SLOTS).astype(jnp.int32)
        + (inner >= 3 * SLOTS).astype(jnp.int32)
    )
    slot = jnp.right_shift(k, 4) * SLOTS + inner - SLOTS * group
    return slot, group


def as_row(column):
    return jnp.transpose(jnp.broadcast_to(column, (column.shape[0], HD)))[0:1, :]


def stream_slots(ids, pass_local):
    rows, width = ids.shape
    stream = iota((PAD, width), 0)
    spread = jnp.zeros((PAD, width), F32)
    place = jnp.full((PAD, width), -1, jnp.int32)
    for r in range(rows):
        inside = (stream >= r * width) & (stream < (r + 1) * width)
        spread = jnp.where(inside, ids[r : r + 1, :].astype(F32), spread)
        place = jnp.where(inside, stream - r * width, place)
    hit = place == iota((PAD, width), 1)
    passage = jnp.sum(jnp.where(hit, spread, 0.0), axis=1, keepdims=True)
    real = iota((PAD, 1), 0) < rows * width
    owner = jnp.floor((passage + 0.5) * (1.0 / pass_local))
    local = jnp.where(real, passage - owner * pass_local, 0.0)
    owner = jnp.where(real, owner, -1.0)
    same = owner == as_row(owner)
    earlier = iota((PAD, PAD), 1) < iota((PAD, PAD), 0)
    position = jnp.sum(jnp.where(same & earlier, 1.0, 0.0), axis=1, keepdims=True)
    return jnp.where(real, owner * SLOTS + position, -1.0), local


def remote(src, dst, send, recv, device):
    return pltpu.make_async_remote_copy(
        src_ref=src, dst_ref=dst, send_sem=send, recv_sem=recv, device_id=device, device_id_type=MESH
    )


def exchange_copy(k, me, tp, stores, msg, recv, send_sem, recv_sem):
    to = lax.rem(me + k, stores)
    return remote(
        msg.at[pl.ds(pl.multiple_of(to * BLOCK, BLOCK), BLOCK)],
        recv.at[pl.ds(pl.multiple_of(me * BLOCK, BLOCK), BLOCK)],
        send_sem.at[k],
        recv_sem.at[k],
        (to, tp),
    )


def route_kernel(stores, pass_local, q_ref, id_ref, recv_ref, wide_ref, msg_ref, send_sem, recv_sem):
    me, tp = lax.axis_index("store"), lax.axis_index("tp")
    barrier = pltpu.get_barrier_semaphore()

    def greet(k, carry):
        pl.semaphore_signal(
            barrier, inc=1, device_id=(lax.rem(me + k, stores), tp), device_id_type=MESH
        )
        return carry

    lax.fori_loop(1, stores, greet, 0)
    streams, width = q_ref.shape
    slot, local = stream_slots(id_ref[...], pass_local)
    wide_ref[...] = jnp.zeros(wide_ref.shape, BF)
    wide_ref[0:streams, 0:width] = q_ref[...]
    wide_ref[:, width:] = jnp.broadcast_to(local, (PAD, HD)).astype(BF)
    rows = stores * BLOCK
    row_slot, row_group = row_parts(iota((rows, 1), 0))
    wanted = jnp.where(row_group < 3, row_slot, -2).astype(F32)
    pick = jnp.where(wanted == as_row(slot), 1.0, 0.0).astype(BF)
    message = dot(pick, wide_ref[:, 2 * WIDE : 3 * WIDE])
    message = jnp.where(row_group == 1, dot(pick, wide_ref[:, WIDE : 2 * WIDE]), message)
    message = jnp.where(row_group == 0, dot(pick, wide_ref[:, 0:WIDE]), message)
    msg_ref[...] = message.astype(BF)
    pl.semaphore_wait(barrier, stores - 1)

    def start(k, carry):
        exchange_copy(k, me, tp, stores, msg_ref, recv_ref, send_sem, recv_sem).start()
        return carry

    lax.fori_loop(1, stores, start, 0)
    mine = pl.ds(pl.multiple_of(me * BLOCK, BLOCK), BLOCK)
    recv_ref[mine, :] = msg_ref[mine, :]

    def finish(k, carry):
        exchange_copy(k, me, tp, stores, msg_ref, recv_ref, send_sem, recv_sem).wait()
        return carry

    lax.fori_loop(1, stores, finish, 0)


def attend_kernel(n_chunks, recv_ref, kv_ref, back_ref, sorted_ref, result_ref):
    rows = recv_ref.shape[0]
    places = sorted_ref.shape[0]
    pass_local = kv_ref.shape[1]
    _, group = row_parts(iota((rows, 1), 0))
    passage = recv_ref[:, 2 * HD : 3 * HD].astype(F32)
    lane = iota((rows, HD), 1).astype(F32)
    member = jnp.where((group == 2) & (passage == lane), 1.0, 0.0)
    lower = jnp.where(iota((rows, rows), 1) < iota((rows, rows), 0), 1.0, 0.0).astype(BF)
    rank = dot(lower, member.astype(BF))
    counts = jnp.sum(member, axis=0, keepdims=True)
    chunks = jnp.floor((counts + (CHUNK - 1)) * (1.0 / CHUNK))
    upto = jnp.where(iota((HD, HD), 0) <= iota((HD, HD), 1), 1.0, 0.0).astype(BF)
    ends = dot(jnp.broadcast_to(chunks, (8, HD)).astype(BF), upto)[0:1, :]
    firsts = ends - chunks
    place = jnp.sum(member * (rank + CHUNK * firsts), axis=1, keepdims=True)
    one = pltpu.roll(jnp.broadcast_to(place, (rows, HD)), rows - SLOTS, 0)
    two = pltpu.roll(jnp.broadcast_to(place, (rows, HD)), rows - 2 * SLOTS, 0)
    place = jnp.where(group == 0, two, jnp.where(group == 1, one, place))
    place = jnp.where(group < 3, place, -1.0)
    place_row = jnp.transpose(place)[0:1, :]
    _, group_row = row_parts(iota((1, rows), 1))
    target = iota((places, 1), 0).astype(F32)
    for g in range(3):
        pick = jnp.where(target == jnp.where(group_row == g, place_row, -2.0), 1.0, 0.0).astype(BF)
        sorted_ref[:, g * WIDE : (g + 1) * WIDE] = dot(pick, recv_ref[...]).astype(BF)
    result_ref[n_chunks * CHUNK :, :] = jnp.zeros(
        (places - n_chunks * CHUNK, result_ref.shape[1]), BF
    )
    limits = jnp.where(iota((1, HD), 1) < pass_local, ends, 1e9)
    lanes = iota((CHUNK, HD), 1)
    head_lane = jnp.bitwise_and(lanes, GROUP - 1)

    def attend(c, carry):
        index = jnp.sum(jnp.where(limits <= c.astype(F32), 1.0, 0.0)).astype(jnp.int32)
        index = jnp.minimum(index, pass_local - 1)
        at = pl.ds(pl.multiple_of(c * CHUNK, CHUNK), CHUNK)
        queries = jnp.concatenate(
            [sorted_ref[at, h * HD : (h + 1) * HD] for h in range(GROUP)], axis=0
        )
        scores = lax.dot_general(
            queries, kv_ref[0, index], (((1,), (1,)), ((), ())), preferred_element_type=F32
        )
        highest = jnp.max(scores, axis=1, keepdims=True)
        terms = jnp.exp2((scores - highest) * (SCALE * 1.4426950408889634))
        total = jnp.sum(terms, axis=1, keepdims=True)
        mixed = dot(terms.astype(BF), kv_ref[1, index]) * (1.0 / total)
        lse = highest * SCALE + jnp.log(total)
        sums = jnp.zeros((CHUNK, HD), F32)
        for h in range(GROUP):
            part = slice(h * CHUNK, (h + 1) * CHUNK)
            result_ref[at, h * HD : (h + 1) * HD] = mixed[part].astype(BF)
            sums = jnp.where(head_lane == h, lse[part], sums)
        high = sums.astype(BF).astype(F32)
        middle = (sums - high).astype(BF).astype(F32)
        low = sums - high - middle
        sums = jnp.where(lanes < GROUP, high, jnp.where(lanes < 2 * GROUP, middle, low))
        result_ref[at, GROUP * HD :] = sums.astype(BF)
        return carry

    lax.fori_loop(0, n_chunks, attend, 0, unroll=4)
    home = jnp.where(
        jnp.broadcast_to(place[:, 0:1], (rows, places)) == iota((rows, places), 1).astype(F32),
        1.0,
        0.0,
    ).astype(BF)
    back = dot(home, result_ref[:, 2 * WIDE : 3 * WIDE])
    back = jnp.where(group == 1, dot(home, result_ref[:, WIDE : 2 * WIDE]), back)
    back = jnp.where(group == 0, dot(home, result_ref[:, 0:WIDE]), back)
    back_ref[...] = back.astype(BF)


def project_kernel(
    stores,
    tps,
    y_chips,
    pass_local,
    q_ref,
    new_ref,
    id_ref,
    back_ref,
    w_ref,
    res_ref,
    out_ref,
    home,
    block,
    weight,
    part,
    others,
    total,
    final,
    ex_send,
    ex_recv,
    w_send,
    w_recv,
    right_send,
    right_recv,
    left_send,
    left_recv,
    sum_send,
    sum_recv,
    end_send,
    end_recv,
):
    me, tp = lax.axis_index("store"), lax.axis_index("tp")
    zs = stores // y_chips
    z = lax.div(me, y_chips)
    y = me - z * y_chips
    streams, width = q_ref.shape
    w_cols = w_ref.shape[1]
    cut = width // tps
    diagonal = z == tp
    barrier = pltpu.get_barrier_semaphore()

    def greet(device):
        pl.semaphore_signal(barrier, inc=1, device_id=device, device_id_type=MESH)

    def greet_store(k, carry):
        greet((lax.rem(me + k, stores), tp))
        return carry

    lax.fori_loop(1, stores, greet_store, 0)
    for k in range(1, tps):
        greet((me, lax.rem(tp + k, tps)))
    for other in range(tps):

        @pl.when(jnp.logical_not(diagonal & (tp == other)))
        def _():
            greet((tp * y_chips + y, other))

    pl.semaphore_wait(barrier, stores + 2 * tps - 2 - diagonal.astype(jnp.int32))

    def start(k, carry):
        exchange_copy(k, me, tp, stores, back_ref, home, ex_send, ex_recv).start()
        return carry

    lax.fori_loop(1, stores, start, 0)
    weight_copies = []
    for k in range(1, y_chips):
        copy = remote(
            w_ref,
            weight.at[y],
            w_send.at[k],
            w_recv.at[k],
            (z * y_chips + lax.rem(y + k, y_chips), tp),
        )
        copy.start()
        weight_copies.append(copy)
    mine = pl.ds(pl.multiple_of(me * BLOCK, BLOCK), BLOCK)
    home[mine, :] = back_ref[mine, :]
    weight[y] = w_ref[...]

    slot, _ = stream_slots(id_ref[...], pass_local)
    rows = stores * BLOCK
    row_slot, row_group = row_parts(iota((1, rows), 1))
    match = slot[0:streams] == row_slot.astype(F32)
    picks = [jnp.where(match & (row_group == g), 1.0, 0.0).astype(BF) for g in range(3)]
    new_key = new_ref[0].astype(F32)
    new_value = new_ref[1].astype(F32)
    own = [
        jnp.sum(q_ref[:, h * HD : (h + 1) * HD].astype(F32) * new_key, axis=1, keepdims=True)
        * SCALE
        for h in range(GROUP)
    ]

    def finish(k, carry):
        exchange_copy(k, me, tp, stores, back_ref, home, ex_send, ex_recv).wait()
        return carry

    lax.fori_loop(1, stores, finish, 0)
    got = [dot(pick, home[...]) for pick in picks]
    sums = got[2][:, 2 * HD : 3 * HD]
    for h in range(GROUP):
        g, b = divmod(h, 3)
        lse = sums[:, h : h + 1] + sums[:, GROUP + h : GROUP + h + 1]
        lse = lse + sums[:, 2 * GROUP + h : 2 * GROUP + h + 1]
        highest = jnp.maximum(lse, own[h])
        first = jnp.exp(lse - highest)
        second = jnp.exp(own[h] - highest)
        mixed = got[g][:, b * HD : (b + 1) * HD] * first + new_value * second
        block[z, :, h * HD : (h + 1) * HD] = (mixed * (1.0 / (first + second))).astype(BF)

    n_right, n_left = zs // 2, (zs - 1) // 2
    to_right = (lax.rem(z + 1, zs) * y_chips + y, tp)
    to_left = (lax.rem(z + zs - 1, zs) * y_chips + y, tp)

    def going_right(k):
        at = block.at[lax.rem(z + zs - k, zs)]
        return remote(at, at, right_send.at[k], right_recv.at[k], to_right)

    def going_left(k):
        at = block.at[lax.rem(z + k, zs)]
        return remote(at, at, left_send.at[k], left_recv.at[k], to_left)

    def came_right(k):
        at = block.at[lax.rem(z + zs - k - 1, zs)]
        return remote(at, at, right_send.at[k], right_recv.at[k], to_right)

    def came_left(k):
        at = block.at[lax.rem(z + k + 1, zs)]
        return remote(at, at, left_send.at[k], left_recv.at[k], to_left)

    if n_right:
        going_right(0).start()
    if n_left:
        going_left(0).start()
    for copy in weight_copies:
        copy.wait_recv()

    def sum_copy(i, k):
        to = lax.rem(tp + k, tps)
        return remote(
            part.at[i, to], others.at[i, tp], sum_send.at[i, k], sum_recv.at[i, k], (me, to)
        )

    def multiply(i, z_of):
        for v in range(y_chips):
            product = dot(block[z_of], weight[v])
            for u in range(w_cols // cut):
                part[i, v * (w_cols // cut) + u] = product[:, u * cut : (u + 1) * cut].astype(BF)
        for k in range(1, tps):
            sum_copy(i, k).start()

    def end_copy(i, z_of):
        return remote(
            total.at[i], final.at[tp], end_send.at[i], end_recv.at[tp], (z_of * y_chips + y, z)
        )

    def add_up(i, z_of):
        for k in range(1, tps):
            sum_copy(i, k).wait_recv()
        value = part[i, tp].astype(F32)
        for k in range(1, tps):
            value = value + others[i, lax.rem(tp + tps - k, tps)].astype(F32)
        total[i] = value.astype(BF)
        if i == 0:

            @pl.when(diagonal)
            def _():
                final[tp] = total[i]

            @pl.when(jnp.logical_not(diagonal))
            def _():
                end_copy(i, z_of).start()

        else:
            end_copy(i, z_of).start()

    order = [0]
    for k in range(1, n_right + 1):
        order.append(-k)
        if k <= n_left:
            order.append(k)
    where = [lax.rem(z + zs + o, zs) for o in order]
    lag = 2
    for i, o in enumerate(order):
        if o < 0:
            came_right(-o - 1).wait_recv()
            if -o < n_right:
                going_right(-o).start()
        elif o > 0:
            came_left(o - 1).wait_recv()
            if o < n_left:
                going_left(o).start()
        multiply(i, where[i])
        if i >= lag:
            add_up(i - lag, where[i - lag])
    for i in range(max(len(order) - lag, 0), len(order)):
        add_up(i, where[i])

    for other in range(tps):

        @pl.when(jnp.logical_not(diagonal & (tp == other)))
        def _():
            remote(
                total.at[0], final.at[other], end_send.at[0], end_recv.at[other], (me, tp)
            ).wait_recv()

        at = slice(other * cut, (other + 1) * cut)
        out_ref[:, at] = (res_ref[:, at].astype(F32) + final[other].astype(F32)).astype(BF)

    for copy in weight_copies:
        copy.wait_send()
    for k in range(n_right):
        going_right(k).wait_send()
    for k in range(n_left):
        going_left(k).wait_send()
    for i in range(zs):
        for k in range(1, tps):
            sum_copy(i, k).wait_send()
        if i == 0:

            @pl.when(jnp.logical_not(diagonal))
            def _():
                end_copy(i, where[i]).wait_send()

        else:
            end_copy(i, where[i]).wait_send()


def params(collective_id=None):
    return pltpu.CompilerParams(
        collective_id=collective_id,
        has_side_effects=collective_id is not None,
        vmem_limit_bytes=40 * 2**20,
    )


def shards(y_chips, query, new_kv, kv_store, passage_ids, residual_in, out_weight):
    stores, tps = lax.axis_size("store"), lax.axis_size("tp")
    zs = stores // y_chips
    streams, width = query.shape
    pass_local = kv_store.shape[1]
    rows = stores * BLOCK
    dma = pltpu.SemaphoreType.DMA
    received = pl.pallas_call(
        functools.partial(route_kernel, stores, pass_local),
        out_shape=jax.ShapeDtypeStruct((rows, WIDE), BF),
        in_specs=[VMEM] * 2,
        out_specs=VMEM,
        scratch_shapes=[
            pltpu.VMEM((PAD, 3 * WIDE), BF),
            pltpu.VMEM((rows, WIDE), BF),
            dma((stores,)),
            dma((stores,)),
        ],
        compiler_params=params(0),
        name="route",
    )(query, passage_ids)
    slots = stores * SLOTS
    n_chunks = (slots + pass_local * (CHUNK - 1)) // CHUNK
    places = -(-n_chunks * CHUNK // HD) * HD
    back = pl.pallas_call(
        functools.partial(attend_kernel, n_chunks),
        out_shape=jax.ShapeDtypeStruct((rows, WIDE), BF),
        in_specs=[VMEM] * 2,
        out_specs=VMEM,
        scratch_shapes=[
            pltpu.VMEM((places, 3 * WIDE), BF),
            pltpu.VMEM((places, 3 * WIDE), BF),
        ],
        compiler_params=params(),
        name="attend",
    )(received, kv_store)
    cut = width // tps
    return pl.pallas_call(
        functools.partial(project_kernel, stores, tps, y_chips, pass_local),
        out_shape=jax.ShapeDtypeStruct((streams, width), BF),
        in_specs=[VMEM] * 6,
        out_specs=VMEM,
        scratch_shapes=[
            pltpu.VMEM((rows, WIDE), BF),
            pltpu.VMEM((zs, streams, width), BF),
            pltpu.VMEM((y_chips, *out_weight.shape), BF),
            pltpu.VMEM((zs, tps, streams, cut), BF),
            pltpu.VMEM((zs, tps, streams, cut), BF),
            pltpu.VMEM((zs, streams, cut), BF),
            pltpu.VMEM((tps, streams, cut), BF),
            dma((stores,)),
            dma((stores,)),
            dma((y_chips,)),
            dma((y_chips,)),
            dma((zs,)),
            dma((zs,)),
            dma((zs,)),
            dma((zs,)),
            dma((zs, tps)),
            dma((zs, tps)),
            dma((zs,)),
            dma((tps,)),
        ],
        compiler_params=params(1),
        name="project",
    )(query, new_kv, passage_ids, back, out_weight, residual_in)


def solution(mesh, y_chips=Y_CHIPS):
    placed = (
        P("store", "tp"),
        P(None, "store", "tp"),
        P(None, "store", None, "tp"),
        P("store", None),
        P("store", "tp"),
        P("tp", "store"),
    )
    return jax.shard_map(
        functools.partial(shards, y_chips),
        mesh=mesh,
        in_specs=placed,
        out_specs=P("store", "tp"),
        check_vma=False,
    )
```

time: 265 us -> 103 us (0.39)
  the two profiles are of different devices: /device:TPU:8 before, /device:TPU:4 now
where the time goes in v1:
time: 103 us
  Pallas kernels  97.9 us (95%)
  local copies, waits for them, and re-layouts  4.76 us (5%)
    pallas_call x1, Pallas kernels, shards(): pl.pallas_call(functools.partial(project_kernel, stores, tps, y_chips, pa...  65.4 us
    pallas_call x1, Pallas kernels, shards(): pl.pallas_call(functools.partial(route_kernel, stores, pass_local), out_s...  20.7 us
    pallas_call x1, Pallas kernels, shards(): pl.pallas_call(functools.partial(attend_kernel, n_chunks), out_shape=jax....  11.8 us
    unnamed x13, local copies, waits for them, and re-layouts  4.76 us

profile of v1, /device:TPU:4, one launch (start us, length us, event | category | flops | bytes accessed | tf_op | source)
XLA Modules:
  0.0 102.7 jit_solution(12145841983731303708)
XLA Ops:
  0.0 0.0 copy-start.1
  0.0 0.9 copy-done.1
  0.9 0.0 copy-start.5
  0.9 0.7 copy-done.5
  1.6 0.0 copy-start.2
  1.6 20.7 %route.1.recv_ref = bf16[512,384]{1,0:T(8,128)(2,1)S(1)} custom-call(bf16[80,1024]{1,0:T(8,128)(2,1)S(1)} %copy-done.1, s32[8,10]{1,0:T(8,128)S(1)} %copy-done.5), custom_call_target="tpu_custom_call" | custom-call | tf_op jit(solution)/shard_map/route/pallas_call | solution.py:444
  22.3 0.0 copy-start
  22.3 2.5 %copy-done = bf16[2,20,512,128]{3,2,1,0:T(8,128)(2,1)S(1)} copy-done((bf16[2,20,512,128]{3,2,1,0:T(8,128)(2,1)S(1)}, bf16[2,20,512,128]{3,2,1,0:T(8,128)(2,1)}, u32[]{:S(2)}) %copy-start) | copy-done | bytes 5242904
  24.8 0.0 copy-start.3
  24.8 0.0 copy-start.4
  24.8 11.8 %attend.1.back_ref = bf16[512,384]{1,0:T(8,128)(2,1)S(1)} custom-call(bf16[512,384]{1,0:T(8,128)(2,1)S(1)} %route.1.recv_ref, bf16[2,20,512,128]{3,2,1,0:T(8,128)(2,1)S(1)} %copy-done), custom_call_target="tpu_custom_call" | custom-call | tf_op jit(solution)/shard_map/attend/pallas_call | solution.py:461
  36.6 0.0 copy-done.2
  36.6 0.0 copy-done.3
  36.7 0.0 copy-done.4
  36.7 65.4 %project.1 = bf16[80,1024]{1,0:T(8,128)(2,1)S(1)} custom-call(bf16[80,1024]{1,0:T(8,128)(2,1)S(1)} %copy-done.1, bf16[2,80,128]{2,1,0:T(8,128)(2,1)S(1)} %copy-done.4, s32[8,10]{1,0:T(8,128)S(1)} %copy-done.5, bf16[512,384]{1,0:T(8,128)(2,1)S(1)} %attend.1.back_ref, bf16[1024,256]{1,0:T(8,128)(2,1)S(1)} %copy-done.2, bf16[80,1024]{1,0:T(8,128)(2,1)S(1)} %copy-done.3), custom_call_target="tpu_custom_call" | custom-call | tf_op jit(solution)/shard_map/project/pallas_call | solution.py:474
  102.0 0.7 copy.8
Async XLA Ops:
  0.0 0.9 copy-start.1
  0.9 0.7 copy-start.5
  1.6 35.0 %copy-start.2 = (bf16[1024,256]{1,0:T(8,128)(2,1)S(1)}, bf16[1024,256]{1,0:T(8,128)(2,1)}, u32[]{:S(2)}) copy-start(bf16[1024,256]{1,0:T(8,128)(2,1)} %w_ref.1) | copy-start | bytes 1572868
  22.3 2.5 %copy-start = (bf16[2,20,512,128]{3,2,1,0:T(8,128)(2,1)S(1)}, bf16[2,20,512,128]{3,2,1,0:T(8,128)(2,1)}, u32[]{:S(2)}) copy-start(bf16[2,20,512,128]{3,2,1,0:T(8,128)(2,1)} %kv_ref.1) | copy-start | bytes 15728644
  24.8 11.9 %copy-start.3 = (bf16[80,1024]{1,0:T(8,128)(2,1)S(1)}, bf16[80,1024]{1,0:T(8,128)(2,1)}, u32[]{:S(2)}) copy-start(bf16[80,1024]{1,0:T(8,128)(2,1)} %res_ref.1) | copy-start | bytes 491524
  24.8 11.9 %copy-start.4 = (bf16[2,80,128]{2,1,0:T(8,128)(2,1)S(1)}, bf16[2,80,128]{2,1,0:T(8,128)(2,1)}, u32[]{:S(2)}) copy-start(bf16[2,80,128]{2,1,0:T(8,128)(2,1)} %new_ref.1) | copy-start | bytes 122884
